TPU v7x, 256 devices: a whole 4x4x8 slice. The times are simulated.
256 devices in a mesh: blk: 128 (over z_hi, y, x, core), head: 2 (over z_lo).
Axes of the slice: x: 4, y: 4, z: 8 (z_hi: 4, z_lo: 2; z = z_hi * 2 + z_lo), core: 2. Of those that a mesh axis runs over, the one named last changes fastest.
Arguments:
- cells: bfloat16 [65536, 256], P('blk', 'head'), may hold values from -6 to 6
- w_query: bfloat16 [256, 256], P(None, 'head'), may hold values from -0.375 to 0.375
- w_key: bfloat16 [256, 256], P(None, 'head'), may hold values from -0.375 to 0.375
- w_value: bfloat16 [256, 256], P(None, 'head'), may hold values from -0.375 to 0.375
- w_source: bfloat16 [2, 256, 256], P(None, None, 'head'), may hold values from -0.375 to 0.375
- w_target: bfloat16 [2, 256, 256], P(None, None, 'head'), may hold values from -0.375 to 0.375
- msg_bias: float32 [2, 256], P(None, 'head'), may hold values from -3 to 3
- w_out: bfloat16 [256, 256], P('head'), may hold values from -0.375 to 0.375
- nbr_block: int32 [512, 4], P('blk'), may hold values from 0 to 511, as said below
- edge_src: int32 [65536, 8], P('blk'), may hold values from 0 to 511
- key_blocks: int32 [512, 32], P('blk'), may hold values from 0 to 511, as said below
Outputs:
- updated: bfloat16 [65536, 256], P('blk', 'head')
Inputs may be any that keep to these rules, and one draw needn't show every extreme that they name: `nbr_block`: the source blocks listed for a destination block lie in its own partition of 4 consecutive blocks or in the partition just before or after it on the loop of 128 partitions. `key_blocks`: each row lists 32 key blocks from 32 different partitions; among all key blocks listed by the 4 query blocks of one partition, those that lie in one partition are the same block.
All inputs are finite; a program needn't handle non-finite values.
Results may differ from a plain program's by a relative error of at most 0.0015.
The roundings to bfloat16 on the way count: a program that leaves them out, or rounds other values in their place, can miss the bound.
Values may be sent and summed in bfloat16 or wider, within the bound.
No kernel may reach another device: no remote copies, remote signals or barrier semaphores. Data moves between devices by JAX's collectives and lax.ppermute only.
A program may use at most 128 MiB of HBM per device.

v0:
```python
import jax
import jax.numpy as jnp
from jax import lax
from jax.sharding import PartitionSpec as P

HEAD_DIM = 32
BLOCK = 128


def padded(value, sides, width):
    for axis, dim in sides:
        peers, length = (lax.axis_size(axis), value.shape[dim])
        up = [(i, (i + 1) % peers) for i in range(peers)]
        down = [(j, i) for i, j in up]
        last = lax.slice_in_dim(value, length - width, length, axis=dim)
        initial = lax.slice_in_dim(value, 0, width, axis=dim)
        before = lax.ppermute(last, axis, up)
        after = lax.ppermute(initial, axis, down)
        value = jnp.concatenate([before, value, after], axis=dim)
    return value


def body(
    cells,
    w_query,
    w_key,
    w_value,
    w_source,
    w_target,
    msg_bias,
    w_out,
    nbr_block,
    edge_src,
    key_blocks,
):
    rows = cells.shape[0]
    width = w_query.shape[1]
    heads_here = width // HEAD_DIM
    blk_dev = rows // BLOCK
    nparts = lax.axis_size("blk")
    edge_count = edge_src.shape[1]
    scale = HEAD_DIM ** (-0.5)
    whole = lax.all_gather(cells, "head", axis=1, tiled=True)
    queries = jnp.dot(whole, w_query, preferred_element_type=jnp.float32).astype(jnp.bfloat16)
    keys = jnp.dot(whole, w_key, preferred_element_type=jnp.float32).astype(jnp.bfloat16)
    values = jnp.dot(whole, w_value, preferred_element_type=jnp.float32).astype(jnp.bfloat16)
    source = jnp.einsum("cd,gdk->cgk", whole, w_source, preferred_element_type=jnp.float32)
    source = source.astype(jnp.bfloat16).reshape(rows, 2 * width)
    target = (
        jnp.einsum("cd,gdk->cgk", whole, w_target, preferred_element_type=jnp.float32)
        + msg_bias[None]
    )
    window = padded(source, (("blk", 0),), rows)
    mine = lax.axis_index("blk")
    own_block = jnp.arange(rows, dtype=jnp.int32) // BLOCK
    src_block = nbr_block[own_block[:, None], edge_src // BLOCK]
    offset = (src_block // blk_dev - mine + 1) % nparts
    window_row = offset * rows + src_block % blk_dev * BLOCK + edge_src % BLOCK
    fetched = jnp.take(window, window_row.reshape(-1), axis=0).reshape(rows, edge_count, 2, width)
    pre = fetched.astype(jnp.float32) + target[:, None]
    message = jax.nn.sigmoid(pre[:, :, 0]) * jax.nn.silu(pre[:, :, 1])
    aggregate = jnp.mean(message, axis=1)
    query_heads = queries.reshape(rows, heads_here, HEAD_DIM)
    part_of = key_blocks // blk_dev
    local_of = key_blocks % blk_dev

    def tile(carry, key_piece, value_piece, first):
        source_part = first // rows
        hit = part_of == source_part
        chosen_local = jnp.max(jnp.where(hit, local_of, -1))
        query_uses = jnp.any(hit, axis=1)
        numer, total = carry
        begin = jnp.maximum(chosen_local, 0) * BLOCK
        block_keys = lax.dynamic_slice_in_dim(key_piece, begin, BLOCK, 0)
        block_values = lax.dynamic_slice_in_dim(value_piece, begin, BLOCK, 0)
        row_mask = jnp.repeat(query_uses, BLOCK).astype(jnp.float32)
        scores = (
            jnp.einsum(
                "qhd,khd->hqk",
                query_heads,
                block_keys.reshape(BLOCK, heads_here, HEAD_DIM),
                preferred_element_type=jnp.float32,
            )
            * scale
        )
        weight = jnp.exp(scores) * row_mask[None, :, None]
        total = total + jnp.sum(weight, axis=2)
        added = jnp.einsum(
            "hqk,khd->qhd",
            weight.astype(jnp.bfloat16),
            block_values.reshape(BLOCK, heads_here, HEAD_DIM),
            preferred_element_type=jnp.float32,
        )
        return (numer + added.reshape(rows, width), total)

    initial = (jnp.zeros((rows, width), jnp.float32), jnp.zeros((heads_here, rows), jnp.float32))
    carry = initial
    key_piece = lax.all_gather(keys, "blk", axis=0, tiled=True)
    value_piece = lax.all_gather(values, "blk", axis=0, tiled=True)
    count = key_piece.shape[0]

    def advance(state, turn):
        first = turn * rows
        part_keys = lax.dynamic_slice_in_dim(key_piece, first, rows, 0)
        part_values = lax.dynamic_slice_in_dim(value_piece, first, rows, 0)
        return (tile(state, part_keys, part_values, first), None)

    carry, unused = lax.scan(advance, carry, jnp.arange(count // rows, dtype=jnp.int32))
    numer, total = carry
    mixed = (numer / jnp.repeat(jnp.transpose(total), HEAD_DIM, axis=1)).astype(jnp.bfloat16)
    partial_out = jnp.dot(mixed, w_out, preferred_element_type=jnp.float32)
    attended = lax.psum_scatter(partial_out, "head", scatter_dimension=1, tiled=True)
    return (cells.astype(jnp.float32) + aggregate + attended).astype(jnp.bfloat16)


def solution(mesh):
    in_specs = (
        P("blk", "head"),
        P(None, "head"),
        P(None, "head"),
        P(None, "head"),
        P(None, None, "head"),
        P(None, None, "head"),
        P(None, "head"),
        P("head", None),
        P("blk", None),
        P("blk", None),
        P("blk", None),
    )
    out_specs = P("blk", "head")
    return jax.shard_map(body, mesh=mesh, in_specs=in_specs, out_specs=out_specs, check_vma=False)
```

profile of v0, /device:TPU:1, one launch (start us, length us, event | category | flops | bytes accessed | tf_op | source)
XLA Modules:
  0.0 1106.5 jit_solution(5081986127554945908)
XLA Ops:
  6.5 5.9 all_gather.9
  12.4 1.7 convolution_convert_fusion.2
  14.2 1.7 convolution_convert_fusion.1
  17.5 3.3 collective-permute-start
  21.6 34.6 %gather_fusion = s32[4096]{0:T(1024)S(1)} fusion(s32[4,4]{1,0:T(4,128)S(1)} %copy-done.1, s32[4096]{0:T(1024)S(1)} %reshape.116), kind=kCustom, calls=%fused_computation | custom fusion | bytes 65536 | tf_op jit(solution)/shard_map/gather | solution.py:56
  59.5 14.6 %gather_fusion.1 = bf16[4096,256]{1,0:T(8,128)(2,1)S(1)} fusion(bf16[1536,256]{1,0:T(8,128)(2,1)S(1)} %pad_maximum_fusion, s32[4096]{0:T(1024)S(1)} %broadcast_clamp_fusion), kind=kCustom, calls=%fused_computation.1 | custom fusion | bytes 4210688 | tf_op jit(solution)/shard_map/jit(_take)/gather | solution.py:59
  74.1 54.5 %all-gather.3.cloned.1.call-done = bf16[65536,128]{1,0:T(8,128)(2,1)} async-done(((bf16[512,128]{1,0:T(8,128)(2,1)}), bf16[65536,128]{1,0:T(8,128)(2,1)}) %all-gather.3.cloned.1.call-update) | async-done | bytes 16777232 | tf_op jit(solution)/shard_map/all_gather | solution.py:99
  128.6 118.2 %all-gather.5.cloned.1.call-done = bf16[65536,128]{1,0:T(8,128)(2,1)} async-done(((bf16[512,128]{1,0:T(8,128)(2,1)}), bf16[65536,128]{1,0:T(8,128)(2,1)}) %all-gather.5.cloned.1.call-update) | async-done | bytes 16777232 | tf_op jit(solution)/shard_map/all_gather | solution.py:98
  247.3 824.6 %while.15 = (s32[]{:T(128)}, f32[512,128]{0,1:T(8,128)S(1)}, f32[4,512]{1,0:T(4,128)S(1)}, s32[128]{0:T(128)}, s32[4,32]{1,0:T(4,128)}, /*index=5*/s32[4,32]{1,0...) while((s32[]{:T(128)}, f32[512,128]{0,1:T(8,128)S(1)}, ...), condition=%wide.region_5.6_spmd.clone, body=%wide.region_1.5_spmd.clone.sunk | while | flops 34736664 | bytes 2594593 | solution.py:108
  249.9 1.3 select_reduce_fusion.2
  256.4 1.3 select_reduce_fusion.2
  269.3 1.3 select_reduce_fusion.2
  275.7 1.3 select_reduce_fusion.2
  282.1 1.3 select_reduce_fusion.2
  288.6 1.3 select_reduce_fusion.2
  295.0 1.3 select_reduce_fusion.2
  301.5 1.3 select_reduce_fusion.2
  307.9 1.3 select_reduce_fusion.2
  314.4 1.3 select_reduce_fusion.2
  320.8 1.3 select_reduce_fusion.2
  327.2 1.3 select_reduce_fusion.2
  333.7 1.3 select_reduce_fusion.2
  340.1 1.3 select_reduce_fusion.2
  346.6 1.3 select_reduce_fusion.2
  353.0 1.3 select_reduce_fusion.2
  359.4 1.3 select_reduce_fusion.2
  365.9 1.3 select_reduce_fusion.2
  372.3 1.3 select_reduce_fusion.2
  378.8 1.3 select_reduce_fusion.2
  385.2 1.3 select_reduce_fusion.2
  391.7 1.3 select_reduce_fusion.2
  398.1 1.3 select_reduce_fusion.2
  404.6 1.3 select_reduce_fusion.2
  411.0 1.3 select_reduce_fusion.2
  417.4 1.3 select_reduce_fusion.2
  423.9 1.3 select_reduce_fusion.2
  430.3 1.3 select_reduce_fusion.2
  436.8 1.3 select_reduce_fusion.2
  443.2 1.3 select_reduce_fusion.2
  449.6 1.3 select_reduce_fusion.2
  456.1 1.3 select_reduce_fusion.2
  462.5 1.3 select_reduce_fusion.2
  469.0 1.3 select_reduce_fusion.2
  475.4 1.3 select_reduce_fusion.2
  481.9 1.3 select_reduce_fusion.2
  488.3 1.3 select_reduce_fusion.2
  494.7 1.3 select_reduce_fusion.2
  501.2 1.3 select_reduce_fusion.2
  507.6 1.3 select_reduce_fusion.2
  514.1 1.3 select_reduce_fusion.2
  520.5 1.3 select_reduce_fusion.2
  527.0 1.3 select_reduce_fusion.2
  533.4 1.3 select_reduce_fusion.2
  539.8 1.3 select_reduce_fusion.2
  546.3 1.3 select_reduce_fusion.2
  552.7 1.3 select_reduce_fusion.2
  559.2 1.3 select_reduce_fusion.2
  565.6 1.3 select_reduce_fusion.2
  572.0 1.3 select_reduce_fusion.2
  1072.0 1.9 fusion.38
  1073.9 2.5 convert_add_fusion
  1076.4 1.9 fusion.11
  1078.4 19.9 %reduce-scatter.2.cloned.1.call-done = f32[512,128]{1,0:T(8,128)} async-done(((f32[512,256]{1,0:T(8,128)}), f32[512,128]{1,0:T(8,128)}) %reduce-scatter.2.cloned.1.call-update) | async-done | bytes 262160 | tf_op jit(solution)/shard_map/reduce_scatter | solution.py:112
  1098.3 1.7 add_convert_fusion
  (1531 shorter events, 600.9 us)
Async XLA Ops:
  6.5 50.6 %copy-start = (bf16[2,256,128]{2,1,0:T(8,128)(2,1)S(1)}, bf16[2,256,128]{2,1,0:T(8,128)(2,1)}, u32[]{:S(2)}) copy-start(bf16[2,256,128]{2,1,0:T(8,128)(2,1)} %param.18) | copy-start | bytes 393220
  6.5 14.5 %copy-start.4 = (s32[512,8]{0,1:T(8,128)S(1)}, s32[512,8]{0,1:T(8,128)}, u32[]{:S(2)}) copy-start(s32[512,8]{0,1:T(8,128)} %param.22) | copy-start | bytes 49156
  6.5 122.1 %all-gather.3.cloned.1.call-start = ((), (), s32[]{:S(2)}) async-start(), calls=%async_computation.1 | async-start | bytes 16908288 | tf_op jit(solution)/shard_map/all_gather | solution.py:99
  14.2 7.4 copy-start.1
  14.2 232.6 %all-gather.5.cloned.1.call-start = ((), (), s32[]{:S(2)}) async-start(), calls=%async_computation.2 | async-start | bytes 16908288 | tf_op jit(solution)/shard_map/all_gather | solution.py:98
  16.0 1082.3 %reduce-scatter.2.cloned.1.call-start = ((), (), s32[]{:S(2)}) async-start(), calls=%async_computation.3 | async-start | bytes 786432 | tf_op jit(solution)/shard_map/reduce_scatter | solution.py:112
  17.5 41.9 %collective-permute-start = (bf16[512,256]{1,0:T(8,128)(2,1)S(1)}, bf16[512,256]{1,0:T(8,128)(2,1)S(1)}, u32[]{:S(2)}, u32[]{:S(2)}) collective-permute-start(bf16[512,256]{1,0:T(8,128)(2,1)S(1)} %copy.28), channel_id=1, source_target_pairs={{0,2},{2,4},{4,6},{6,8},{8,10},{10,12},{12,14},{14,16},{16,18},{18... | collective-permute-start | bytes 786440 | tf_op jit(solution)/shard_map/ppermute | solution.py:17
  20.8 38.7 %collective-permute-start.1 = (bf16[512,256]{1,0:T(8,128)(2,1)S(1)}, bf16[512,256]{1,0:T(8,128)(2,1)S(1)}, u32[]{:S(2)}, u32[]{:S(2)}) collective-permute-start(bf16[512,256]{1,0:T(8,128)(2,1)S(1)} %copy.28), channel_id=1, source_target_pairs={{2,0},{4,2},{6,4},{8,6},{10,8},{12,10},{14,12},{16,14},{18,16},{20... | collective-permute-start | bytes 786440 | tf_op jit(solution)/shard_map/ppermute | solution.py:18
  21.5 35.6 %copy-start.6 = (f32[2,128]{1,0:T(2,128)S(1)}, f32[2,128]{1,0:T(2,128)}, u32[]{:S(2)}) copy-start(f32[2,128]{1,0:T(2,128)} %param.19) | copy-start | bytes 3076
  56.2 1.2 copy-start.5
  56.2 3.0 copy-start.3
  1076.4 21.9 %copy-start.2 = (bf16[512,128]{1,0:T(8,128)(2,1)S(1)}, bf16[512,128]{1,0:T(8,128)(2,1)}, u32[]{:S(2)}) copy-start(bf16[512,128]{1,0:T(8,128)(2,1)} %param.13) | copy-start | bytes 393220
Sparse Core Ops, SparseCore 0:
  14.3 114.2 all-gather.2
  132.2 114.5 all-gather.4
  1074.0 24.2 reduce-scatter.1
where the time goes:
time: 1120 us; the launch traced here: 1110 us
  local copies, waits for them, and re-layouts  348 us (31%)
  other arithmetic  291 us (26%)
  waiting for transfers between devices  193 us (17%)
  loops' own time  164 us (15%)
  matrix products  88.2 us (8%)
  between operations  13.4 us (1%)
    reduce_max x128, other arithmetic, tile(): chosen_local = jnp.max(jnp.where(hit, local_of, -1))  169 us
    another operation x1, loops' own time, body(): lax.scan(advance, carry, jnp.arange(count // rows, dtype=jnp.int32))  164 us
    dynamic_slice x128, local copies, waits for them, and re-layouts, body(): lax.scan(advance, carry, jnp.arange(count // rows, dtype=jnp.int32))  155 us
    all_gather x1, waiting for transfers between devices, body(): key_piece = lax.all_gather(keys, 'blk', axis=0, tiled=True)  118 us
    dynamic_slice x256, local copies, waits for them, and re-layouts, tile(): block_keys = lax.dynamic_slice_in_dim(key_piece, begin, BLOCK, 0)  118 us
    reduce_or x128, other arithmetic, tile(): query_uses = jnp.any(hit, axis=1)  102 us
    dot_general x128, matrix products, tile(): jnp.einsum('qhd,khd->hqk', query_heads, block_keys.reshape(BLOCK, heads_h...  55.5 us
    all_gather x1, waiting for transfers between devices, body(): value_piece = lax.all_gather(values, 'blk', axis=0, tiled=True)  54.5 us
  transfers between devices with their start and end apart: 5, of which 3 were waited for; matrix products, arithmetic and copies ran while one was open for 5% of the time, Pallas kernels for 0%

commit v1 on v0

--- a/solution.py
+++ b/solution.py
@@ -96,7 +96,9 @@
     initial = (jnp.zeros((rows, width), jnp.float32), jnp.zeros((heads_here, rows), jnp.float32))
     carry = initial
     key_piece = lax.all_gather(keys, "blk", axis=0, tiled=True)
-    value_piece = lax.all_gather(values, "blk", axis=0, tiled=True)
+    value_piece = jnp.concatenate(
+        lax.all_to_all(jnp.stack([values] * lax.axis_size("blk")), "blk", 0, 0), axis=0
+    )
     count = key_piece.shape[0]
 
     def advance(state, turn):

time: 1120 us -> 1370 us (1.22)
  waiting for transfers between devices: 193 us -> 401 us
  local copies, waits for them, and re-layouts: 348 us -> 383 us
  other arithmetic: 291 us -> 275 us
  starting transfers between devices: 3.6 us -> 19.2 us
    all_to_all x0 -> x1, waiting for transfers between devices: none -> 317 us  [body(): lax.all_to_all(jnp.stack([values] * lax.axis_size('blk')), 'blk', 0, 0)]
    all_gather x1, waiting for transfers between devices: 118 us -> 0.01 us  [body(): key_piece = lax.all_gather(keys, 'blk', axis=0, tiled=True)]
    all_gather x1 -> x0, waiting for transfers between devices: 54.5 us -> none  [body(): value_piece = lax.all_gather(values, 'blk', axis=0, tiled=True)]
    ppermute x1, waiting for transfers between devices: 0.01 us -> 47.1 us  [padded(): before = lax.ppermute(last, axis, up)]
    all_to_all x0 -> x1, local copies, waits for them, and re-layouts: none -> 21.9 us  [body(): lax.all_to_all(jnp.stack([values] * lax.axis_size('blk')), 'blk', 0, 0)]
    all_to_all x0 -> x1, starting transfers between devices: none -> 17.4 us  [body(): lax.all_to_all(jnp.stack([values] * lax.axis_size('blk')), 'blk', 0, 0)]
  transfers between devices with their start and end apart: 5 -> 5, of which waited for: 3 -> 4; matrix products, arithmetic and copies ran while one was open for 5% -> 6% of each run, Pallas kernels for 0% -> 0%
where the time goes in v1:
time: 1370 us; the launch traced here: 1350 us
  waiting for transfers between devices  401 us (29%)
  local copies, waits for them, and re-layouts  383 us (28%)
  other arithmetic  275 us (20%)
  loops' own time  170 us (12%)
  matrix products  86.9 us (6%)
  starting transfers between devices  19.2 us (1%)
    all_to_all x1, waiting for transfers between devices, body(): lax.all_to_all(jnp.stack([values] * lax.axis_size('blk')), 'blk', 0, 0)  317 us
    another operation x1, loops' own time, body(): lax.scan(advance, carry, jnp.arange(count // rows, dtype=jnp.int32))  170 us
    dynamic_slice x128, local copies, waits for them, and re-layouts, body(): lax.scan(advance, carry, jnp.arange(count // rows, dtype=jnp.int32))  162 us
    reduce_max x128, other arithmetic, tile(): chosen_local = jnp.max(jnp.where(hit, local_of, -1))  161 us
    dynamic_slice x256, local copies, waits for them, and re-layouts, tile(): block_keys = lax.dynamic_slice_in_dim(key_piece, begin, BLOCK, 0)  118 us
    reduce_or x128, other arithmetic, tile(): query_uses = jnp.any(hit, axis=1)  95.2 us
    dot_general x128, matrix products, tile(): jnp.einsum('qhd,khd->hqk', query_heads, block_keys.reshape(BLOCK, heads_h...  55.7 us
    ppermute x1, waiting for transfers between devices, padded(): before = lax.ppermute(last, axis, up)  47.1 us
  transfers between devices with their start and end apart: 5, of which 4 were waited for; matrix products, arithmetic and copies ran while one was open for 6% of the time, Pallas kernels for 0%

profile of v1, /device:TPU:1, one launch (start us, length us, event | category | flops | bytes accessed | tf_op | source)
XLA Modules:
  0.0 1353.9 jit_solution(8704449814182419153)
XLA Ops:
  6.5 5.9 all_gather.6
  13.6 6.0 stack.2
  19.7 17.4 %all-to-all-start = ((bf16[128,512,128]{1,2,0:T(8,128)(2,1)}), bf16[128,512,128]{1,2,0:T(8,128)(2,1)}, u32[]{:S(2)}, u32[]{:S(2)}) async-start(bf16[128,512,128]{1,2,0:T(8,128)(2,1)} %stack.2), calls=%async_computation | async-start | bytes 33554432 | tf_op jit(solution)/shard_map/all_to_all | solution.py:100
  38.7 1.7 collective-permute-start
  40.9 34.6 %gather_fusion = s32[4096]{0:T(1024)S(1)} fusion(s32[4,4]{1,0:T(4,128)S(1)} %copy-done.1, s32[4096]{0:T(1024)S(1)} %reshape.122), kind=kCustom, calls=%fused_computation | custom fusion | bytes 65536 | tf_op jit(solution)/shard_map/gather | solution.py:56
  78.7 47.1 %collective-permute-done = bf16[512,256]{1,0:T(8,128)(2,1)S(1)} collective-permute-done((bf16[512,256]{1,0:T(8,128)(2,1)S(1)}, bf16[512,256]{1,0:T(8,128)(2,1)S(1)}, u32[]{:S(2)}, u32[]{:S(2)}) %collective-permute-start) | collective-permute-done | bytes 262176 | tf_op jit(solution)/shard_map/ppermute | solution.py:17
  125.9 10.8 collective-permute-done.1
  136.8 14.6 %gather_fusion.1 = bf16[4096,256]{1,0:T(8,128)(2,1)S(1)} fusion(bf16[1536,256]{1,0:T(8,128)(2,1)S(1)} %pad_maximum_fusion, s32[4096]{0:T(1024)S(1)} %broadcast_clamp_fusion), kind=kCustom, calls=%fused_computation.1 | custom fusion | bytes 4210688 | tf_op jit(solution)/shard_map/jit(_take)/gather | solution.py:59
  151.4 316.8 %all-to-all-done = bf16[128,512,128]{1,2,0:T(8,128)(2,1)} async-done(((bf16[128,512,128]{1,2,0:T(8,128)(2,1)}), bf16[128,512,128]{1,2,0:T(8,128)(2,1)}, u32[]{:S(2)}, u32[]{:S(2)}) %all-to-all-start) | async-done | bytes 16777248 | tf_op jit(solution)/shard_map/all_to_all | solution.py:100
  468.2 21.9 %copy.60 = bf16[128,512,128]{2,1,0:T(8,128)(2,1)} copy(bf16[128,512,128]{1,2,0:T(8,128)(2,1)} %all-to-all-done) | data formatting | bytes 33554432 | tf_op jit(solution)/shard_map/all_to_all | solution.py:100
  490.6 822.5 %while.15 = (s32[]{:T(128)}, f32[512,128]{0,1:T(8,128)S(1)}, f32[4,512]{1,0:T(4,128)S(1)}, s32[128]{0:T(128)}, s32[4,32]{1,0:T(4,128)}, /*index=5*/s32[4,32]{1,0...) while((s32[]{:T(128)}, f32[512,128]{0,1:T(8,128)S(1)}, ...), condition=%wide.region_5.6_spmd.clone, body=%wide.region_1.5_spmd.clone.sunk | while | flops 34736664 | bytes 2594593 | solution.py:110
  497.0 1.3 dynamic_slice.35
  503.4 1.3 dynamic_slice.35
  509.9 1.3 dynamic_slice.35
  516.3 1.3 dynamic_slice.35
  522.7 1.3 dynamic_slice.35
  529.1 1.3 dynamic_slice.35
  535.6 1.3 dynamic_slice.35
  548.4 1.3 dynamic_slice.35
  554.8 1.3 dynamic_slice.35
  561.3 1.3 dynamic_slice.35
  567.7 1.3 dynamic_slice.35
  574.1 1.3 dynamic_slice.35
  580.5 1.3 dynamic_slice.35
  587.0 1.3 dynamic_slice.35
  593.4 1.3 dynamic_slice.35
  599.8 1.3 dynamic_slice.35
  606.3 1.3 dynamic_slice.35
  612.7 1.3 dynamic_slice.35
  619.1 1.3 dynamic_slice.35
  625.5 1.3 dynamic_slice.35
  638.4 1.3 dynamic_slice.35
  644.8 1.3 dynamic_slice.35
  651.2 1.3 dynamic_slice.35
  664.1 1.3 dynamic_slice.35
  670.5 1.3 dynamic_slice.35
  676.9 1.3 dynamic_slice.35
  683.4 1.3 dynamic_slice.35
  689.8 1.3 dynamic_slice.35
  702.6 1.3 dynamic_slice.35
  709.1 1.3 dynamic_slice.35
  715.5 1.3 dynamic_slice.35
  721.9 1.3 dynamic_slice.35
  734.8 1.3 dynamic_slice.35
  741.2 1.3 dynamic_slice.35
  747.6 1.3 dynamic_slice.35
  754.1 1.3 dynamic_slice.35
  760.5 1.3 dynamic_slice.35
  773.3 1.3 dynamic_slice.35
  779.8 1.3 dynamic_slice.35
  786.2 1.3 dynamic_slice.35
  799.0 1.3 dynamic_slice.35
  805.5 1.3 dynamic_slice.35
  811.9 1.3 dynamic_slice.35
  818.3 1.3 dynamic_slice.35
  824.7 1.3 dynamic_slice.35
  837.6 1.3 dynamic_slice.35
  844.0 1.3 dynamic_slice.35
  850.4 1.3 dynamic_slice.35
  1313.1 1.9 fusion.38
  1315.0 2.5 convert_add_fusion
  1317.6 1.9 fusion.11
  1319.5 25.9 %reduce-scatter.2.cloned.1.call-done = f32[512,128]{1,0:T(8,128)} async-done(((f32[512,256]{1,0:T(8,128)}), f32[512,128]{1,0:T(8,128)}) %reduce-scatter.2.cloned.1.call-update) | async-done | bytes 262160 | tf_op jit(solution)/shard_map/reduce_scatter | solution.py:114
  1345.4 1.7 add_convert_fusion
  (1537 shorter events, 599.1 us)
Async XLA Ops:
  6.5 69.9 %copy-start = (bf16[2,256,128]{2,1,0:T(8,128)(2,1)S(1)}, bf16[2,256,128]{2,1,0:T(8,128)(2,1)}, u32[]{:S(2)}) copy-start(bf16[2,256,128]{2,1,0:T(8,128)(2,1)} %param.18) | copy-start | bytes 393220
  19.7 17.5 %copy-start.4 = (bf16[256,128]{1,0:T(8,128)(2,1)S(1)}, bf16[256,128]{1,0:T(8,128)(2,1)}, u32[]{:S(2)}) copy-start(bf16[256,128]{1,0:T(8,128)(2,1)} %param.15) | copy-start | bytes 196612
  19.7 18.4 %copy-start.3 = (bf16[2,256,128]{2,1,0:T(8,128)(2,1)S(1)}, bf16[2,256,128]{2,1,0:T(8,128)(2,1)}, u32[]{:S(2)}) copy-start(bf16[2,256,128]{2,1,0:T(8,128)(2,1)} %param.17) | copy-start | bytes 393220
  19.7 448.6 %all-to-all-start = ((bf16[128,512,128]{1,2,0:T(8,128)(2,1)}), bf16[128,512,128]{1,2,0:T(8,128)(2,1)}, u32[]{:S(2)}, u32[]{:S(2)}) async-start(bf16[128,512,128]{1,2,0:T(8,128)(2,1)} %stack.2), calls=%async_computation | async-start | bytes 33554432 | tf_op jit(solution)/shard_map/all_to_all | solution.py:100
  37.0 3.3 copy-start.6
  37.1 3.9 copy-start.1
  37.1 453.0 %all-gather.2.cloned.1.call-start = ((), (), s32[]{:S(2)}) async-start(), calls=%async_computation.2 | async-start | bytes 16908288 | tf_op jit(solution)/shard_map/all_gather | solution.py:98
  38.0 1307.3 %reduce-scatter.2.cloned.1.call-start = ((), (), s32[]{:S(2)}) async-start(), calls=%async_computation.3 | async-start | bytes 786432 | tf_op jit(solution)/shard_map/reduce_scatter | solution.py:114
  38.7 87.2 %collective-permute-start = (bf16[512,256]{1,0:T(8,128)(2,1)S(1)}, bf16[512,256]{1,0:T(8,128)(2,1)S(1)}, u32[]{:S(2)}, u32[]{:S(2)}) collective-permute-start(bf16[512,256]{1,0:T(8,128)(2,1)S(1)} %copy.54), channel_id=1, source_target_pairs={{0,2},{2,4},{4,6},{6,8},{8,10},{10,12},{12,14},{14,16},{16,18},{18... | collective-permute-start | bytes 786440 | tf_op jit(solution)/shard_map/ppermute | solution.py:17
  40.4 96.3 %collective-permute-start.1 = (bf16[512,256]{1,0:T(8,128)(2,1)S(1)}, bf16[512,256]{1,0:T(8,128)(2,1)S(1)}, u32[]{:S(2)}, u32[]{:S(2)}) collective-permute-start(bf16[512,256]{1,0:T(8,128)(2,1)S(1)} %copy.54), channel_id=1, source_target_pairs={{2,0},{4,2},{6,4},{8,6},{10,8},{12,10},{14,12},{16,14},{18,16},{20... | collective-permute-start | bytes 786440 | tf_op jit(solution)/shard_map/ppermute | solution.py:18
  40.9 35.6 %copy-start.8 = (f32[2,128]{1,0:T(2,128)S(1)}, f32[2,128]{1,0:T(2,128)}, u32[]{:S(2)}) copy-start(f32[2,128]{1,0:T(2,128)} %param.19) | copy-start | bytes 3076
  75.5 1.2 copy-start.7
  75.5 3.0 copy-start.5
  1317.6 27.8 %copy-start.2 = (bf16[512,128]{1,0:T(8,128)(2,1)S(1)}, bf16[512,128]{1,0:T(8,128)(2,1)}, u32[]{:S(2)}) copy-start(bf16[512,128]{1,0:T(8,128)(2,1)} %param.13) | copy-start | bytes 393220
Sparse Core Ops, SparseCore 0:
  41.5 315.6 all-gather.1
  1315.2 30.1 reduce-scatter.1
